TPU v7x, 32 devices: a whole 2x2x4 slice. The times are simulated.
32 devices in a mesh: row: 4 (over y, core), col: 8 (over z, x).
Axes of the slice: x: 2, y: 2, z: 4, core: 2. Of those that a mesh axis runs over, the one named last changes fastest.
Arguments:
- node_feats: bfloat16 [4096, 128], P(('row', 'col')), may hold values from -6 to 6
- send_rows: int32 [4, 8, 8, 32], P('row', 'col'), may hold values from 0 to 127
- send_count: int32 [4, 8, 8], P('row', 'col'), may hold values from 8 to 32, as said below
- block_tiles: int32 [4, 8, 4, 5], P('row', 'col'), may hold values from 0 to 1
- block_values: bfloat16 [4, 8, 4, 5, 128, 128], P('row', 'col'), may hold values from 0 to 1, as said below
- w_self: bfloat16 [128, 256], replicated, may hold values from -0.5 to 0.5
- w_neigh: bfloat16 [128, 256], replicated, may hold values from -1 to 1
- bias_term: float32 [256], replicated, may hold values from -3 to 3
- cotangent: bfloat16 [4096, 256], P(('row', 'col')), may hold values from -6 to 6
Outputs:
- hidden: bfloat16 [4096, 256], P(('row', 'col'))
- input_grads: float32 [4096, 128], P(('row', 'col'))
- self_grads: float32 [128, 256], replicated
- neigh_grads: float32 [128, 256], replicated
- bias_grads: float32 [256], replicated
Inputs may be any that keep to these rules, and one draw needn't show every extreme that they name: `send_rows`: slots at or past a list's count carry no data. `send_count`: every sending device fills all 32 slots toward at least one peer. `block_values`: each entry is 0 or 1.
All inputs are finite; a program needn't handle non-finite values.
Results may differ from a plain program's by a relative error of at most 0.0055.
Values may be sent and summed in bfloat16 or wider, within the bound.
A program may use at most 64 MiB of HBM per device.

v0:
```python
import jax
import jax.numpy as jnp
from jax import lax
from jax.sharding import PartitionSpec as P


def inner_rows(left, right):
    return lax.dot_general(
        left, right, (((0,), (0,)), ((), ())), preferred_element_type=jnp.float32
    )


def shards(
    node_feats,
    send_rows,
    send_count,
    block_tiles,
    block_values,
    w_self,
    w_neigh,
    bias_term,
    cotangent,
):
    node_count, in_width = node_feats.shape
    rows_list = send_rows[0, 0]
    peer_counts = send_count[0, 0]
    col_count, slot_count = rows_list.shape
    indices = block_tiles[0, 0]
    values = block_values[0, 0]
    block_rows, block_depth = indices.shape
    tile_count = col_count * slot_count // 128
    live_slots = lax.broadcasted_iota(jnp.int32, (col_count, slot_count), 1) < peer_counts[:, None]
    outgoing = jnp.where(live_slots[:, :, None], node_feats[rows_list], 0.0)
    incoming = lax.all_to_all(outgoing, "col", split_axis=0, concat_axis=0, tiled=True)
    tile_rows = incoming.reshape(tile_count, 128, in_width)
    picked = tile_rows[indices]
    partial_value = jnp.einsum("pkij,pkjf->pif", values, picked, preferred_element_type=jnp.float32)
    partial_value = partial_value.reshape(block_rows * 128, in_width)
    row_degree = jnp.sum(values, axis=(1, 3), dtype=jnp.float32).reshape(-1)
    agg_sum, degree = (
        lax.psum_scatter(partial_value, "row", scatter_dimension=0, tiled=True),
        lax.psum_scatter(row_degree, "row", scatter_dimension=0, tiled=True),
    )
    divisor = jnp.maximum(degree, 1.0)
    neigh_mean = (agg_sum / divisor[:, None]).astype(jnp.bfloat16)
    preact = (
        jnp.dot(node_feats, w_self, preferred_element_type=jnp.float32)
        + jnp.dot(neigh_mean, w_neigh, preferred_element_type=jnp.float32)
        + bias_term
    )
    hidden = jax.nn.silu(preact).astype(jnp.bfloat16)
    sigmoid_pre = jax.nn.sigmoid(preact)
    pre_grads = (
        cotangent.astype(jnp.float32) * sigmoid_pre * (1.0 + preact * (1.0 - sigmoid_pre))
    ).astype(jnp.bfloat16)
    local_sums = (
        inner_rows(node_feats, pre_grads),
        inner_rows(neigh_mean, pre_grads),
        jnp.sum(pre_grads.astype(jnp.float32), axis=0),
    )
    self_grads, neigh_grads, bias_grads = lax.psum(
        (local_sums[0], local_sums[1], local_sums[2]), ("row", "col")
    )
    mean_grads = (
        jnp.dot(pre_grads, w_neigh.T, preferred_element_type=jnp.float32) / divisor[:, None]
    ).astype(jnp.bfloat16)
    panel_grad = lax.all_gather(mean_grads, "row", axis=0, tiled=True)
    blocks = panel_grad.reshape(block_rows, 128, in_width)
    spread_back = jnp.einsum("pkij,pif->pkjf", values, blocks, preferred_element_type=jnp.float32)
    tile_ids = lax.broadcasted_iota(jnp.int32, (block_rows * block_depth, tile_count), 1)
    onehot = (indices.reshape(-1)[:, None] == tile_ids).astype(jnp.float32)
    tile_grads = jnp.einsum(
        "qt,qjf->tjf",
        onehot,
        spread_back.reshape(-1, 128, in_width),
        precision=lax.Precision.HIGHEST,
    )
    tile_grads = tile_grads.reshape(col_count, slot_count, in_width)
    returned = lax.all_to_all(
        tile_grads.astype(jnp.bfloat16), "col", split_axis=0, concat_axis=0, tiled=True
    ).astype(tile_grads.dtype)
    masked = jnp.where(live_slots[:, :, None], returned, 0.0)
    scattered = (
        jnp.zeros((node_count, in_width), jnp.float32)
        .at[rows_list.reshape(-1)]
        .add(masked.reshape(-1, in_width))
    )
    input_grads = jnp.dot(pre_grads, w_self.T, preferred_element_type=jnp.float32) + scattered
    return (hidden, input_grads, self_grads, neigh_grads, bias_grads)


def solution(mesh):
    placed = (
        P(("row", "col"), None),
        P("row", "col", None, None),
        P("row", "col", None),
        P("row", "col", None, None),
        P("row", "col", None, None, None, None),
        P(),
        P(),
        P(),
        P(("row", "col"), None),
    )
    return jax.shard_map(
        shards,
        mesh=mesh,
        in_specs=placed,
        out_specs=(P(("row", "col"), None), P(("row", "col"), None), P(), P(), P()),
        check_vma=False,
    )
```

profile of v0, /device:TPU:0, one launch (start us, length us, event | category | flops | bytes accessed | tf_op | source)
XLA Modules:
  0.0 212.1 jit_solution(1159221192453489061)
XLA Ops:
  7.2 0.8 compare_select_fusion
  8.1 0.7 iota_compare_fusion
  8.8 1.5 gather_fusion
  10.3 0.7 broadcast_select_fusion
  11.0 7.3 %all-to-all-start = ((bf16[8,32,128]{2,1,0:T(8,128)(2,1)}), bf16[8,32,128]{2,1,0:T(8,128)(2,1)S(1)}, u32[]{:S(2)}, u32[]{:S(2)}) async-start(bf16[8,32,128]{2,1,0:T(8,128)(2,1)} %broadcast_select_fusion), calls=%async_computation | async-start | bytes 131072 | tf_op jit(solution)/shard_map/all_to_all | solution.py:34
  18.3 0.8 reshape_squeeze.3
  19.1 0.7 compare_select_fusion.2
  19.8 0.8 eq.10
  20.5 1.3 convert_reduce_fusion
  21.9 0.6 dynamic-slice
  23.1 6.3 %all-reduce = f32[512]{0:T(512)S(1)} all-reduce(f32[512]{0:T(512)S(1)} %bitcast.64), channel_id=3, replica_groups=mesh['row'=4,'col'=8] {'row'}, use_global_device_ids=true, to_apply=%region_2.3.clone | all-reduce | flops 512 | bytes 4096
  29.5 0.7 gather_fusion.1
  30.2 1.0 fusion.4
  31.3 0.1 fusion.11
  31.5 20.9 %reduce-scatter.2.cloned.1.call-done = f32[128,128]{1,0:T(8,128)} async-done(((f32[512,128]{1,0:T(8,128)}), f32[128,128]{1,0:T(8,128)}) %reduce-scatter.2.cloned.1.call-update) | async-done | bytes 65552 | tf_op jit(solution)/shard_map/reduce_scatter | solution.py:41
  52.3 1.7 convert_reduce_fusion.1
  54.1 0.2 fusion.1
  54.2 0.9 convolution_bitcast_fusion
  55.1 5.4 %all_gather.3 = bf16[512,128]{1,0:T(8,128)(2,1)S(1)} all-gather(bf16[128,128]{1,0:T(8,128)(2,1)S(1)} %fusion.1), channel_id=1, replica_groups=mesh['row'=4,'col'=8] {'row'}, dimensions={0}, use_global_device_ids=true | all-gather | bytes 163840 | tf_op jit(solution)/shard_map/all_gather | solution.py:67
  60.5 0.4 fusion.2
  60.9 0.6 copy.22
  61.5 0.6 convolution_convert_fusion
  62.1 0.6 copy.23
  62.7 5.5 %all-to-all-start.1 = ((bf16[8,32,128]{2,1,0:T(8,128)(2,1)}), bf16[8,32,128]{2,1,0:T(8,128)(2,1)S(1)}, u32[]{:S(2)}, u32[]{:S(2)}) async-start(bf16[8,32,128]{2,1,0:T(8,128)(2,1)} %bitcast.18), calls=%async_computation.2 | async-start | bytes 131072 | tf_op jit(solution)/shard_map/all_to_all | solution.py:79
  68.3 0.9 fusion.10
  69.3 0.1 fusion.12
  69.4 39.8 %psum.23 = f32[256]{0:T(256)} all-reduce(f32[256]{0:T(256)S(1)} %get-tuple-element.22), channel_id=1, replica_groups=mesh['row'=4,'col'=8] {'row','col'}, use_global_device_ids=true, to_apply=%region_7.8 | all-reduce | flops 256 | bytes 2048 | tf_op jit(solution)/shard_map/psum | solution.py:61
  109.3 0.1 convert_select_fusion
  109.4 2.0 scatter_fusion
  111.4 90.7 %all-reduce.4.cloned.1.call-done = (f32[128,256]{0,1:T(8,128)}, f32[128,256]{1,0:T(8,128)}) async-done(((f32[128,256]{0,1:T(8,128)}, f32[128,256]{1,0:T(8,128)}), (f32[128,256]{0,1:T(8,128)}, f32[128,256]{1,0:T(8,128)})) %all-reduce.4.cloned.1.call-update) | async-done | bytes 262160 | tf_op jit(solution)/shard_map/psum | solution.py:61
  202.0 1.7 copy.24
  203.7 1.6 copy.32
  (30 shorter events, 0.5 us)
Async XLA Ops:
  7.2 45.2 %copy-start = (bf16[128,256]{1,0:T(8,128)(2,1)S(1)}, bf16[128,256]{1,0:T(8,128)(2,1)}, u32[]{:S(2)}) copy-start(bf16[128,256]{1,0:T(8,128)(2,1)} %param.15) | copy-start | bytes 196612
  7.2 14.7 %copy-start.8 = (u32[32]{0:T(128)S(1)}, u32[32]{0:T(128)}, u32[]{:S(2)}) copy-start(u32[32]{0:T(128)} %constant.25) | copy-start | bytes 388
  7.2 23.0 %copy-start.3 = (bf16[1,1,4,5,128,128]{5,4,3,2,1,0:T(8,128)(2,1)S(1)}, bf16[1,1,4,5,128,128]{5,4,3,2,1,0:T(8,128)(2,1)}, u32[]{:S(2)}) copy-start(bf16[1,1,4,5,128,128]{5,4,3,2,1,0:T(8,128)(2,1)} %param.13) | copy-start | bytes 1966084
  11.0 18.4 %all-to-all-start = ((bf16[8,32,128]{2,1,0:T(8,128)(2,1)}), bf16[8,32,128]{2,1,0:T(8,128)(2,1)S(1)}, u32[]{:S(2)}, u32[]{:S(2)}) async-start(bf16[8,32,128]{2,1,0:T(8,128)(2,1)} %broadcast_select_fusion), calls=%async_computation | async-start | bytes 131072 | tf_op jit(solution)/shard_map/all_to_all | solution.py:34
  18.3 34.1 %reduce-scatter.2.cloned.1.call-start = ((), (), s32[]{:S(2)}) async-start(), calls=%async_computation.3 | async-start | bytes 327680 | tf_op jit(solution)/shard_map/reduce_scatter | solution.py:41
  29.4 1.9 copy-start.2
  29.5 1.9 copy-start.4
  29.5 22.9 %copy-start.6 = (bf16[128,256]{1,0:T(8,128)(2,1)S(1)}, bf16[128,256]{1,0:T(8,128)(2,1)}, u32[]{:S(2)}) copy-start(bf16[128,256]{1,0:T(8,128)(2,1)} %param.17) | copy-start | bytes 196612
  29.5 22.9 %copy-start.7 = (f32[256]{0:T(256)S(1)}, f32[256]{0:T(256)}, u32[]{:S(2)}) copy-start(f32[256]{0:T(256)} %param.16) | copy-start | bytes 3076
  61.5 6.9 %copy-start.5 = (f32[128,128]{1,0:T(8,128)S(1)}, f32[128,128]{1,0:T(8,128)}, u32[]{:S(2)}) copy-start(f32[128,128]{1,0:T(8,128)} %reduce-scatter.2.cloned.1.call-done) | copy-start | bytes 196612
  62.7 46.5 %all-to-all-start.1 = ((bf16[8,32,128]{2,1,0:T(8,128)(2,1)}), bf16[8,32,128]{2,1,0:T(8,128)(2,1)S(1)}, u32[]{:S(2)}, u32[]{:S(2)}) async-start(bf16[8,32,128]{2,1,0:T(8,128)(2,1)} %bitcast.18), calls=%async_computation.2 | async-start | bytes 131072 | tf_op jit(solution)/shard_map/all_to_all | solution.py:79
  68.3 133.8 %all-reduce.4.cloned.1.call-start = ((), (), s32[]{:S(2)}) async-start(), calls=%async_computation.4 | async-start | bytes 524288 | tf_op jit(solution)/shard_map/psum | solution.py:61
  111.4 93.9 %copy-start.1 = (f32[128,128]{1,0:T(8,128)}, f32[128,128]{1,0:T(8,128)S(1)}, u32[]{:S(2)}) copy-start(f32[128,128]{1,0:T(8,128)S(1)} %scatter_fusion) | copy-start | bytes 196612
Sparse Core Ops, SparseCore 0:
  31.3 20.9 reduce-scatter.1
  76.3 125.6 all-reduce.3
where the time goes:
time: 213 us; the launch traced here: 212 us
  waiting for transfers between devices  112 us (53%)
  blocking collectives  51.6 us (24%)
  between operations  14.9 us (7%)
  starting transfers between devices  12.9 us (6%)
  local copies, waits for them, and re-layouts  8.91 us (4%)
  other arithmetic  6.33 us (3%)
  matrix products  5.95 us (3%)
    psum x1, waiting for transfers between devices, shards(): lax.psum((local_sums[0], local_sums[1], local_sums[2]), ('row', 'col'))  90.7 us
    psum x1, blocking collectives, shards(): lax.psum((local_sums[0], local_sums[1], local_sums[2]), ('row', 'col'))  39.8 us
    reduce_scatter x1, waiting for transfers between devices, shards(): lax.psum_scatter(partial_value, 'row', scatter_dimension=0, tiled=True)  20.9 us
    all_to_all x1, starting transfers between devices, shards(): lax.all_to_all(outgoing, 'col', split_axis=0, concat_axis=0, tiled=True)  7.25 us
    unnamed x1, blocking collectives  6.33 us
    all_to_all x1, starting transfers between devices, shards(): lax.all_to_all(tile_grads.astype(jnp.bfloat16), 'col', split_axis=0, conc...  5.53 us
    all_gather x1, blocking collectives, shards(): panel_grad = lax.all_gather(mean_grads, 'row', axis=0, tiled=True)  5.41 us
  transfers between devices with their start and end apart: 4, of which 2 were waited for; matrix products, arithmetic and copies ran while one was open for 4% of the time, Pallas kernels for 0%

commit v1 on v0

v1 whole, which is shorter than its diff:
```python
import functools

import jax
import jax.numpy as jnp
from jax import lax
from jax.experimental import pallas as pl
from jax.experimental.pallas import tpu as pltpu
from jax.sharding import PartitionSpec as P

BF = jnp.bfloat16
F32 = jnp.float32
MESH = pl.DeviceIdType.MESH
PIECE = 16


def mm(left, right, contract=(1, 0)):
    return lax.dot_general(
        left, right, (((contract[0],), (contract[1],)), ((), ())), preferred_element_type=F32
    )


def each(first, count, body):
    if count - first <= 8:
        for step in range(first, count):
            body(step)
    else:
        lax.fori_loop(first, count, lambda step, carry: (body(step), carry)[1], 0)


def rows_at(ref, index, size):
    if not isinstance(index, int):
        return ref.at[pl.ds(pl.multiple_of(index * size, size), size)]
    return ref.at[pl.ds(index * size, size)]


def layer_kernel(
    row_count, col_count,
    feats_h, rows_h, count_h, tiles_h, values_h, w_self_h, w_neigh_h, bias_h, cot_h,
    hidden_o, base_o, grads_o, bias_o,
    feats, rows, count, tiles, values, w_self, w_neigh, bias, cot,
    onehot, outgoing, inbox, weights, weights_t, deg_out, deg_in, part_out, part_in,
    panel, grad_out, grad_in, bias_row, bias_in, bias_col, bias_in2, back_out, back_in,
    piece_out, piece_in,
    load_sem, send_a, recv_a, send_d, recv_d, send_p, recv_p, send_m, recv_m, send_g, recv_g,
    send_b, recv_b, send_t, recv_t, send_c, recv_c, send_h, recv_h, send_x, recv_x, send_y, recv_y,
):
    node_count, in_width = feats.shape
    slot_count = rows.shape[3]
    tile_count = inbox.shape[0] // 128
    depth = tiles.shape[3]
    grad_rows = grads_o.shape[0]
    share = grad_rows // row_count
    piece = max(PIECE, share // col_count)
    owners = share // piece
    r = lax.axis_index("row")
    c = lax.axis_index("col")

    def row_peer(step):
        return lax.rem(r + step, row_count)

    def col_peer(step):
        return lax.rem(c + step, col_count)

    def row_source(step):
        return lax.rem(r + row_count - step, row_count)

    def col_source(step):
        return lax.rem(c + col_count - step, col_count)

    loads = []
    pairs = (
        (rows_h, rows), (count_h, count), (feats_h, feats), (tiles_h, tiles), (values_h, values),
        (w_self_h, w_self), (w_neigh_h, w_neigh), (bias_h, bias), (cot_h, cot),
    )
    for number, (source, target) in enumerate(pairs):
        copy = pltpu.make_async_copy(source, target, load_sem.at[number])
        copy.start()
        loads.append(copy)

    barrier = pltpu.get_barrier_semaphore()
    each(1, row_count, lambda s: pl.semaphore_signal(
        barrier, inc=1, device_id=(row_peer(s), c), device_id_type=MESH))
    each(1, col_count, lambda s: pl.semaphore_signal(
        barrier, inc=1, device_id=(r, col_peer(s)), device_id_type=MESH))

    def remote(source, target, send, recv, device):
        return pltpu.make_async_remote_copy(
            src_ref=source, dst_ref=target, send_sem=send, recv_sem=recv,
            device_id=device, device_id_type=MESH)

    def to_row(step, source, target, send, recv):
        return remote(source, target, send.at[step], recv.at[step], (row_peer(step), c))

    def to_col(step, source, target, send, recv):
        return remote(source, target, send.at[step], recv.at[step], (r, col_peer(step)))

    for copy in loads[:3]:
        copy.wait()
    slot = lax.broadcasted_iota(jnp.int32, (1, slot_count), 1)
    node = lax.broadcasted_iota(jnp.int32, (node_count, slot_count), 0)
    for peer in range(col_count):
        listed = jnp.where(slot < count[0, 0, peer], rows[0, 0, pl.ds(peer, 1), :], -1)
        hot = (node == listed).astype(F32).astype(BF)
        onehot[:, pl.ds(peer * slot_count, slot_count)] = hot
    outgoing[...] = mm(onehot[...], feats[...], (0, 0)).astype(BF)

    pl.semaphore_wait(barrier, row_count + col_count - 2)

    def feature_copy(step):
        return to_col(step, rows_at(outgoing, col_peer(step), slot_count),
                      rows_at(inbox, c, slot_count), send_a, recv_a)

    each(1, col_count, lambda s: feature_copy(s).start())
    rows_at(inbox, c, slot_count)[...] = rows_at(outgoing, c, slot_count)[...]

    loads[3].wait()
    loads[4].wait()
    ones = jnp.ones((8, inbox.shape[0]), BF)

    def merge(block):
        for tile in range(tile_count):
            total = jnp.zeros((128, 128), F32)
            for k in range(depth):
                chosen = (tiles[0, 0, block, k] == tile).astype(F32)
                total += values[0, 0, block, k].astype(F32) * chosen
            merged = total.astype(BF)
            rows_at(weights, block, 128)[:, pl.ds(tile * 128, 128)] = merged
        deg_out[block] = mm(ones, rows_at(weights, block, 128)[...], (1, 1))

    each(0, row_count, merge)

    def degree_copy(step):
        return to_row(step, deg_out.at[row_peer(step)], deg_in.at[r], send_d, recv_d)

    each(1, row_count, lambda s: degree_copy(s).start())
    deg_in[r] = deg_out[r]

    def turn(block):
        start = block * 128 if isinstance(block, int) else pl.multiple_of(block * 128, 128)
        weights_t[:, pl.ds(start, 128)] = rows_at(weights, block, 128)[...].astype(F32).T.astype(BF)

    each(0, row_count, turn)
    for copy in loads[5:]:
        copy.wait()
    own_part = mm(feats[...], w_self[...]) + bias[...]
    each(1, row_count, lambda s: degree_copy(s).wait_recv())
    degree = deg_in[0]
    for other in range(1, row_count):
        degree = degree + deg_in[other]
    inverse = 1.0 / jnp.maximum(degree[0:1, :], 1.0)
    inverse = jnp.broadcast_to(inverse, (128, 128)).T

    each(1, col_count, lambda s: feature_copy(s).wait_recv())

    def partial_copy(step):
        return to_row(step, rows_at(part_out, row_peer(step), 128), part_in.at[r], send_p, recv_p)

    def aggregate(step):
        block = row_peer(step)
        rows_at(part_out, block, 128)[...] = mm(
            rows_at(weights, block, 128)[...], inbox[...]).astype(BF)
        partial_copy(step).start()

    each(1, row_count, aggregate)
    agg_sum = mm(rows_at(weights, r, 128)[...], inbox[...])
    part_in[r] = jnp.zeros((128, in_width), BF)
    each(1, row_count, lambda s: partial_copy(s).wait_recv())
    for other in range(row_count):
        agg_sum = agg_sum + part_in[other].astype(F32)

    neigh_mean = (agg_sum * inverse).astype(BF)
    preact = own_part + mm(neigh_mean, w_neigh[...])
    sigmoid_pre = jax.nn.sigmoid(preact)
    pre_grads = (
        cot[...].astype(F32) * sigmoid_pre * (1.0 + preact * (1.0 - sigmoid_pre))
    ).astype(BF)
    rows_at(panel, r, 128)[...] = (mm(pre_grads, w_neigh[...], (1, 1)) * inverse).astype(BF)

    def panel_copy(step):
        return to_row(step, rows_at(panel, r, 128), rows_at(panel, r, 128), send_m, recv_m)

    each(1, row_count, lambda s: panel_copy(s).start())

    half = grad_out.shape[1]
    for number, left in enumerate((feats[...], neigh_mean)):
        product = mm(left, pre_grads, (0, 0)).astype(BF)
        for side in range(2):
            grad_out[pl.ds((2 * number + side) * in_width, in_width), :] = (
                product[:, side * half:(side + 1) * half])

    def share_copy(step):
        return to_row(step, rows_at(grad_out, row_peer(step), share), grad_in.at[r], send_g, recv_g)

    each(1, row_count, lambda s: share_copy(s).start())
    grad_in[r] = rows_at(grad_out, r, share)[...]
    bias_row[...] = mm(jnp.ones((8, node_count), BF), pre_grads)

    def bias_copy(step):
        return to_row(step, bias_row, bias_in.at[r], send_b, recv_b)

    each(1, row_count, lambda s: bias_copy(s).start())
    bias_in[r] = bias_row[...]
    hidden_o[...] = (preact * sigmoid_pre).astype(BF)
    base = mm(pre_grads, w_self[...], (1, 1))

    each(1, row_count, lambda s: panel_copy(s).wait_recv())
    back_out[...] = mm(weights_t[...], panel[...]).astype(BF)

    def back_copy(step):
        return to_col(step, rows_at(back_out, col_peer(step), slot_count),
                      rows_at(back_in, c, slot_count), send_t, recv_t)

    each(1, col_count, lambda s: back_copy(s).start())
    rows_at(back_in, c, slot_count)[...] = rows_at(back_out, c, slot_count)[...]

    def owning(holder, body):
        if owners == col_count:
            body()
        else:
            pl.when(holder < owners)(body)

    def piece_copy(step):
        return to_col(step, rows_at(piece_out, col_peer(step) % owners, piece),
                      piece_in.at[c], send_c, recv_c)

    each(1, row_count, lambda s: share_copy(s).wait_recv())
    total = grad_in[0].astype(F32)
    for other in range(1, row_count):
        total = total + grad_in[other].astype(F32)
    piece_out[...] = total.astype(BF)
    each(1, col_count, lambda s: owning(col_peer(s), lambda: piece_copy(s).start()))
    piece_in[c] = rows_at(piece_out, c % owners, piece)[...]

    each(1, row_count, lambda s: bias_copy(s).wait_recv())
    bias_total = bias_in[0]
    for other in range(1, row_count):
        bias_total = bias_total + bias_in[other]
    bias_col[...] = bias_total

    def bias_copy2(step):
        return to_col(step, bias_col, bias_in2.at[c], send_h, recv_h)

    each(1, col_count, lambda s: bias_copy2(s).start())
    bias_in2[c] = bias_col[...]

    def final_piece(holder):
        start = r * share + holder * piece
        return grads_o.at[pl.ds(pl.multiple_of(start, piece), piece)]

    def final_copy(step):
        return to_col(step, final_piece(c), final_piece(c), send_x, recv_x)

    def reduce_piece():
        each(1, col_count, lambda s: piece_copy(s).wait_recv())
        whole = piece_in[0].astype(F32)
        for other in range(1, col_count):
            whole = whole + piece_in[other].astype(F32)
        final_piece(c)[...] = whole.astype(BF)
        each(1, col_count, lambda s: final_copy(s).start())

    owning(c, reduce_piece)

    each(1, col_count, lambda s: back_copy(s).wait_recv())
    base_o[...] = base + mm(onehot[...], back_in[...])
    each(1, col_count, lambda s: bias_copy2(s).wait_recv())
    bias_total = bias_in2[0]
    for other in range(1, col_count):
        bias_total = bias_total + bias_in2[other]
    bias_o[...] = bias_total

    each(1, col_count, lambda s: owning(col_source(s), lambda: final_copy(s).wait_recv()))

    def share_final(step):
        own = rows_at(grads_o, r, share)
        return to_row(step, own, own, send_y, recv_y)

    each(1, row_count, lambda s: share_final(s).start())
    each(1, row_count, lambda s: share_final(s).wait_recv())

    for step_copy in (degree_copy, partial_copy, panel_copy, share_copy, bias_copy, share_final):
        each(1, row_count, lambda s: step_copy(s).wait_send())
    for step_copy in (feature_copy, back_copy, bias_copy2):
        each(1, col_count, lambda s: step_copy(s).wait_send())
    each(1, col_count, lambda s: owning(col_peer(s), lambda: piece_copy(s).wait_send()))
    owning(c, lambda: each(1, col_count, lambda s: final_copy(s).wait_send()))


def write_kernel(hidden_i, base_i, grads_i, bias_i, hidden, base, self_grads, neigh_grads, bias):
    hidden[...] = hidden_i[...]
    base[...] = base_i[...]
    rows, width = self_grads.shape
    half = grads_i.shape[1]
    for number, target in enumerate((self_grads, neigh_grads)):
        for side in range(width // half):
            block = grads_i[pl.ds((2 * number + side) * rows, rows), :]
            target[:, pl.ds(side * half, half)] = block.astype(F32)
    bias[...] = bias_i[0:1, :]


def shards(row_count, col_count, node_feats, send_rows, send_count, block_tiles, block_values,
           w_self, w_neigh, bias_term, cotangent):
    nodes, width = node_feats.shape
    hid = w_self.shape[1]
    half = hid // 2
    slots = send_rows.shape[3]
    received = col_count * slots
    panel = row_count * nodes
    grad_rows = 4 * width
    share = grad_rows // row_count
    piece = max(PIECE, share // col_count)
    bias_term = bias_term.reshape(1, hid)
    arrays = (node_feats, send_rows, send_count, block_tiles, block_values, w_self, w_neigh,
              bias_term, cotangent)
    spaces = (pltpu.VMEM, pltpu.VMEM, pltpu.SMEM, pltpu.SMEM) + (pltpu.VMEM,) * 5
    row_sems = pltpu.SemaphoreType.DMA((row_count,))
    col_sems = pltpu.SemaphoreType.DMA((col_count,))
    vmem = pl.BlockSpec(memory_space=pltpu.VMEM)
    scratch = [space(array.shape, array.dtype) for space, array in zip(spaces, arrays)] + [
        pltpu.VMEM((nodes, received), BF),
        pltpu.VMEM((received, width), BF),
        pltpu.VMEM((received, width), BF),
        pltpu.VMEM((panel, received), BF),
        pltpu.VMEM((received, panel), BF),
        pltpu.VMEM((row_count, 8, nodes), F32),
        pltpu.VMEM((row_count, 8, nodes), F32),
        pltpu.VMEM((panel, width), BF),
        pltpu.VMEM((row_count, nodes, width), BF),
        pltpu.VMEM((panel, width), BF),
        pltpu.VMEM((grad_rows, half), BF),
        pltpu.VMEM((row_count, share, half), BF),
        pltpu.VMEM((8, hid), F32),
        pltpu.VMEM((row_count, 8, hid), F32),
        pltpu.VMEM((8, hid), F32),
        pltpu.VMEM((col_count, 8, hid), F32),
        pltpu.VMEM((received, width), BF),
        pltpu.VMEM((received, width), BF),
        pltpu.VMEM((share, half), BF),
        pltpu.VMEM((col_count, piece, half), BF),
        pltpu.SemaphoreType.DMA((len(arrays),)),
        col_sems, col_sems, row_sems, row_sems, row_sems, row_sems, row_sems, row_sems,
        row_sems, row_sems, row_sems, row_sems, col_sems, col_sems, col_sems, col_sems,
        col_sems, col_sems, col_sems, col_sems, row_sems, row_sems,
    ]
    results = pl.pallas_call(
        functools.partial(layer_kernel, row_count, col_count),
        out_shape=(
            jax.ShapeDtypeStruct((nodes, hid), BF),
            jax.ShapeDtypeStruct((nodes, width), F32),
            jax.ShapeDtypeStruct((grad_rows, half), BF),
            jax.ShapeDtypeStruct((8, hid), F32),
        ),
        in_specs=[pl.BlockSpec(memory_space=pl.ANY)] * len(arrays),
        out_specs=(vmem,) * 4,
        scratch_shapes=scratch,
        compiler_params=pltpu.CompilerParams(
            collective_id=0, has_side_effects=True, vmem_limit_bytes=40 * 1024 * 1024),
    )(*arrays)
    hidden, input_grads, self_grads, neigh_grads, bias_grads = pl.pallas_call(
        write_kernel,
        out_shape=(
            jax.ShapeDtypeStruct((nodes, hid), BF),
            jax.ShapeDtypeStruct((nodes, width), F32),
            jax.ShapeDtypeStruct((width, hid), F32),
            jax.ShapeDtypeStruct((width, hid), F32),
            jax.ShapeDtypeStruct((1, hid), F32),
        ),
        in_specs=[vmem] * 4,
        out_specs=(vmem,) * 5,
    )(*results)
    return hidden, input_grads, self_grads, neigh_grads, bias_grads.reshape(hid)


def solution(mesh):
    placed = (
        P(("row", "col"), None),
        P("row", "col", None, None),
        P("row", "col", None),
        P("row", "col", None, None),
        P("row", "col", None, None, None, None),
        P(),
        P(),
        P(),
        P(("row", "col"), None),
    )
    return jax.shard_map(
        functools.partial(shards, mesh.shape["row"], mesh.shape["col"]),
        mesh=mesh,
        in_specs=placed,
        out_specs=(P(("row", "col"), None), P(("row", "col"), None), P(), P(), P()),
        check_vma=False,
    )
```

time: 213 us -> 42.4 us (0.20)
  waiting for transfers between devices: 112 us -> 0 us
  blocking collectives: 51.6 us -> 0 us
  Pallas kernels: 0 us -> 32.4 us
  between operations: 14.9 us -> 0.68 us
  starting transfers between devices: 12.9 us -> 0 us
  other arithmetic: 6.33 us -> 0 us
  matrix products: 5.95 us -> 0 us
    psum x1 -> x0, waiting for transfers between devices: 90.7 us -> none  [shards(): lax.psum((local_sums[0], local_sums[1], local_sums[2]), ('row', 'col'))]
    psum x1 -> x0, blocking collectives: 39.8 us -> none  [shards(): lax.psum((local_sums[0], local_sums[1], local_sums[2]), ('row', 'col'))]
    pallas_call x0 -> x2, Pallas kernels: none -> 32.4 us  [the longest x1 30.7 us: shards(): pl.pallas_call(functools.partial(layer_kernel, row_count, col_count), out...]
    reduce_scatter x1 -> x0, waiting for transfers between devices: 20.9 us -> none  [shards(): lax.psum_scatter(partial_value, 'row', scatter_dimension=0, tiled=True)]
    all_to_all x2 -> x0, starting transfers between devices: 12.8 us -> none  [the longest x1 7.25 us: shards(): lax.all_to_all(outgoing, 'col', split_axis=0, concat_axis=0, tiled=True)]
    unnamed x1 -> x0, blocking collectives: 6.33 us -> none
    dot_general x9 -> x0, matrix products: 5.95 us -> none  [the longest x2 1.79 us: inner_rows(): lax.dot_general(left, right, (((0,), (0,)), ((), ())), preferred_element_...]
    all_gather x1 -> x0, blocking collectives: 5.41 us -> none  [shards(): panel_grad = lax.all_gather(mean_grads, 'row', axis=0, tiled=True)]
  transfers between devices with their start and end apart: 4 -> 0, of which waited for: 2 -> 0; matrix products, arithmetic and copies ran while one was open for 4% -> 0% of each run, Pallas kernels for 0% -> 0%
where the time goes in v1:
time: 42.4 us; the launch traced here: 42 us
  Pallas kernels  32.4 us (76%)
  local copies, waits for them, and re-layouts  8.88 us (21%)
  between operations  0.68 us (2%)
    pallas_call x1, Pallas kernels, shards(): pl.pallas_call(functools.partial(layer_kernel, row_count, col_count), out...  30.7 us
    unnamed x26, local copies, waits for them, and re-layouts  8.88 us
    pallas_call x1, Pallas kernels, shards(): pl.pallas_call(write_kernel, out_shape=(jax.ShapeDtypeStruct((nodes, hid)...  1.73 us

profile of v1, /device:TPU:0, one launch (start us, length us, event | category | flops | bytes accessed | tf_op | source)
XLA Modules:
  0.0 42.0 jit_solution(3332790800575045603)
XLA Ops:
  0.6 0.0 copy-start.11
  0.6 0.0 copy-start.12
  0.7 0.7 %copy-done.11 = f32[256]{0:T(256)S(1)} copy-done((f32[256]{0:T(256)S(1)}, f32[256]{0:T(256)}, u32[]{:S(2)}) %copy-start.11) | copy-done | bytes 1048
  1.3 0.0 copy-done.12
  1.3 0.0 copy-start
  1.3 1.1 %copy-done = bf16[1,1,4,5,128,128]{5,4,3,2,1,0:T(8,128)(2,1)S(1)} copy-done((bf16[1,1,4,5,128,128]{5,4,3,2,1,0:T(8,128)(2,1)S(1)}, bf16[1,1,4,5,128,128]{5,4,3,2,1,0:T(8,128)(2,1)}, u32[]{:S(2)}) %copy-start) | copy-done | bytes 655384
  2.4 0.0 copy-start.4
  2.4 0.8 %copy-done.4 = bf16[128,256]{1,0:T(8,128)(2,1)S(1)} copy-done((bf16[128,256]{1,0:T(8,128)(2,1)S(1)}, bf16[128,256]{1,0:T(8,128)(2,1)}, u32[]{:S(2)}) %copy-start.4) | copy-done | bytes 65560
  3.2 0.0 copy-start.5
  3.2 0.8 %copy-done.5 = bf16[128,256]{1,0:T(8,128)(2,1)S(1)} copy-done((bf16[128,256]{1,0:T(8,128)(2,1)S(1)}, bf16[128,256]{1,0:T(8,128)(2,1)}, u32[]{:S(2)}) %copy-start.5) | copy-done | bytes 65560
  4.1 0.0 copy-start.6
  4.1 0.8 %copy-done.6 = bf16[128,256]{1,0:T(8,128)(2,1)S(1)} copy-done((bf16[128,256]{1,0:T(8,128)(2,1)S(1)}, bf16[128,256]{1,0:T(8,128)(2,1)}, u32[]{:S(2)}) %copy-start.6) | copy-done | bytes 65560
  4.9 0.0 copy-start.7
  4.9 0.8 %copy-done.7 = bf16[128,128]{1,0:T(8,128)(2,1)S(1)} copy-done((bf16[128,128]{1,0:T(8,128)(2,1)S(1)}, bf16[128,128]{1,0:T(8,128)(2,1)}, u32[]{:S(2)}) %copy-start.7) | copy-done | bytes 32792
  5.7 0.0 copy-start.9
  5.7 0.7 %copy-done.9 = s32[1,1,8,32]{3,2,1,0:T(8,128)S(1)} copy-done((s32[1,1,8,32]{3,2,1,0:T(8,128)S(1)}, s32[1,1,8,32]{3,2,1,0:T(8,128)}, u32[]{:S(2)}) %copy-start.9) | copy-done | bytes 1048
  6.4 0.0 copy-start.10
  6.4 0.7 %copy-done.10 = s32[1,1,4,5]{3,2,1,0:T(4,128)S(1)} copy-done((s32[1,1,4,5]{3,2,1,0:T(4,128)S(1)}, s32[1,1,4,5]{3,2,1,0:T(4,128)}, u32[]{:S(2)}) %copy-start.10) | copy-done | bytes 104
  7.1 30.7 %shard_map.128 = (bf16[128,256]{1,0:T(8,128)(2,1)S(1)}, f32[128,128]{1,0:T(8,128)S(1)}, bf16[512,128]{1,0:T(8,128)(2,1)S(1)}, f32[8,256]{1,0:T(8,128)S(1)}) custom-call(bf16[128,128]{1,0:T(8,128)(2,1)S(1)} %copy-done.7, s32[1,1,8,32]{3,2,1,0:T(8,128)S(1)} %copy-done.9, s32[1,1,8]{2,1,0:T(1,128)S(1)} %copy-done.12, s32[1,1,4,5]{3,2,1,0:T(4,128)S(1)} %copy-done.10, ...), custom_call_target="tpu_custom_call" | custom-call | tf_op jit(solution)/shard_map/pallas_call | solution.py:344
  37.7 0.0 copy-start.1
  37.7 0.6 %copy-done.1 = bf16[512,128]{1,0:T(8,128)(2,1)} copy-done((bf16[512,128]{1,0:T(8,128)(2,1)}, bf16[512,128]{1,0:T(8,128)(2,1)S(1)}, u32[]{:S(2)}) %copy-start.1) | copy-done | bytes 131096
  38.4 0.0 copy-start.2
  38.4 0.6 %copy-done.2 = bf16[128,256]{1,0:T(8,128)(2,1)} copy-done((bf16[128,256]{1,0:T(8,128)(2,1)}, bf16[128,256]{1,0:T(8,128)(2,1)S(1)}, u32[]{:S(2)}) %copy-start.2) | copy-done | bytes 65560
  39.0 0.0 copy-start.3
  39.0 0.6 %copy-done.3 = f32[128,128]{1,0:T(8,128)} copy-done((f32[128,128]{1,0:T(8,128)}, f32[128,128]{1,0:T(8,128)S(1)}, u32[]{:S(2)}) %copy-start.3) | copy-done | bytes 65560
  39.6 0.0 copy-start.8
  39.6 0.6 %copy-done.8 = f32[8,256]{1,0:T(8,128)} copy-done((f32[8,256]{1,0:T(8,128)}, f32[8,256]{1,0:T(8,128)S(1)}, u32[]{:S(2)}) %copy-start.8) | copy-done | bytes 8216
  40.2 1.7 %shard_map.129 = (bf16[128,256]{1,0:T(8,128)(2,1)}, f32[128,128]{1,0:T(8,128)}, f32[128,256]{1,0:T(8,128)}, f32[128,256]{1,0:T(8,128)}, f32[1,256]{1,0:T(1,128)}) custom-call(bf16[128,256]{1,0:T(8,128)(2,1)} %copy-done.2, f32[128,128]{1,0:T(8,128)} %copy-done.3, bf16[512,128]{1,0:T(8,128)(2,1)} %copy-done.1, f32[8,256]{1,0:T(8,128)} %copy-done.8), custom_call_target="tpu_custom_call" | custom-call | tf_op jit(solution)/shard_map/pallas_call | solution.py:358
Async XLA Ops:
  0.6 0.7 %copy-start.11 = (f32[256]{0:T(256)S(1)}, f32[256]{0:T(256)}, u32[]{:S(2)}) copy-start(f32[256]{0:T(256)} %param.16) | copy-start | bytes 3076
  0.6 0.7 %copy-start.12 = (s32[1,1,8]{2,1,0:T(1,128)S(1)}, s32[1,1,8]{2,1,0:T(1,128)}, u32[]{:S(2)}) copy-start(s32[1,1,8]{2,1,0:T(1,128)} %count_h.1) | copy-start | bytes 100
  1.3 1.1 %copy-start = (bf16[1,1,4,5,128,128]{5,4,3,2,1,0:T(8,128)(2,1)S(1)}, bf16[1,1,4,5,128,128]{5,4,3,2,1,0:T(8,128)(2,1)}, u32[]{:S(2)}) copy-start(bf16[1,1,4,5,128,128]{5,4,3,2,1,0:T(8,128)(2,1)} %values_h.1) | copy-start | bytes 1966084
  2.4 0.8 %copy-start.4 = (bf16[128,256]{1,0:T(8,128)(2,1)S(1)}, bf16[128,256]{1,0:T(8,128)(2,1)}, u32[]{:S(2)}) copy-start(bf16[128,256]{1,0:T(8,128)(2,1)} %w_self_h.1) | copy-start | bytes 196612
  3.2 0.8 %copy-start.5 = (bf16[128,256]{1,0:T(8,128)(2,1)S(1)}, bf16[128,256]{1,0:T(8,128)(2,1)}, u32[]{:S(2)}) copy-start(bf16[128,256]{1,0:T(8,128)(2,1)} %w_neigh_h.1) | copy-start | bytes 196612
  4.1 0.8 %copy-start.6 = (bf16[128,256]{1,0:T(8,128)(2,1)S(1)}, bf16[128,256]{1,0:T(8,128)(2,1)}, u32[]{:S(2)}) copy-start(bf16[128,256]{1,0:T(8,128)(2,1)} %cot_h.1) | copy-start | bytes 196612
  4.9 0.8 %copy-start.7 = (bf16[128,128]{1,0:T(8,128)(2,1)S(1)}, bf16[128,128]{1,0:T(8,128)(2,1)}, u32[]{:S(2)}) copy-start(bf16[128,128]{1,0:T(8,128)(2,1)} %feats_h.1) | copy-start | bytes 98308
  5.7 0.7 %copy-start.9 = (s32[1,1,8,32]{3,2,1,0:T(8,128)S(1)}, s32[1,1,8,32]{3,2,1,0:T(8,128)}, u32[]{:S(2)}) copy-start(s32[1,1,8,32]{3,2,1,0:T(8,128)} %rows_h.1) | copy-start | bytes 3076
  6.4 0.7 %copy-start.10 = (s32[1,1,4,5]{3,2,1,0:T(4,128)S(1)}, s32[1,1,4,5]{3,2,1,0:T(4,128)}, u32[]{:S(2)}) copy-start(s32[1,1,4,5]{3,2,1,0:T(4,128)} %tiles_h.1) | copy-start | bytes 244
  37.7 0.7 %copy-start.1 = (bf16[512,128]{1,0:T(8,128)(2,1)}, bf16[512,128]{1,0:T(8,128)(2,1)S(1)}, u32[]{:S(2)}) copy-start(bf16[512,128]{1,0:T(8,128)(2,1)S(1)} %get-tuple-element.16.grads_i) | copy-start | bytes 393220
  38.4 0.6 %copy-start.2 = (bf16[128,256]{1,0:T(8,128)(2,1)}, bf16[128,256]{1,0:T(8,128)(2,1)S(1)}, u32[]{:S(2)}) copy-start(bf16[128,256]{1,0:T(8,128)(2,1)S(1)} %get-tuple-element.14.hidden_i) | copy-start | bytes 196612
  39.0 0.6 %copy-start.3 = (f32[128,128]{1,0:T(8,128)}, f32[128,128]{1,0:T(8,128)S(1)}, u32[]{:S(2)}) copy-start(f32[128,128]{1,0:T(8,128)S(1)} %get-tuple-element.15.base_i) | copy-start | bytes 196612
  39.6 0.6 %copy-start.8 = (f32[8,256]{1,0:T(8,128)}, f32[8,256]{1,0:T(8,128)S(1)}, u32[]{:S(2)}) copy-start(f32[8,256]{1,0:T(8,128)S(1)} %get-tuple-element.17.bias_i) | copy-start | bytes 24580

commit v2 on v1

--- a/solution.py
+++ b/solution.py
@@ -20,7 +20,7 @@
 
 
 def each(first, count, body):
-    if count - first <= 8:
+    if count - first <= 32:
         for step in range(first, count):
             body(step)
     else:
@@ -42,7 +42,7 @@
     panel, grad_out, grad_in, bias_row, bias_in, bias_col, bias_in2, back_out, back_in,
     piece_out, piece_in,
     load_sem, send_a, recv_a, send_d, recv_d, send_p, recv_p, send_m, recv_m, send_g, recv_g,
-    send_b, recv_b, send_t, recv_t, send_c, recv_c, send_h, recv_h, send_x, recv_x, send_y, recv_y,
+    send_b, recv_b, send_t, recv_t, send_c, recv_c, send_h, recv_h, send_x, recv_x, send_y, recv_y, send_z, recv_z,
 ):
     node_count, in_width = feats.shape
     slot_count = rows.shape[3]
@@ -52,6 +52,8 @@
     share = grad_rows // row_count
     piece = max(PIECE, share // col_count)
     owners = share // piece
+    total_count = row_count * col_count
+    direct = total_count * PIECE == grad_rows
     r = lax.axis_index("row")
     c = lax.axis_index("col")
 
@@ -61,8 +63,13 @@
     def col_peer(step):
         return lax.rem(c + step, col_count)
 
-    def row_source(step):
-        return lax.rem(r + row_count - step, row_count)
+    me = r * col_count + c
+
+    def any_peer(step):
+        return lax.rem(me + step, total_count)
+
+    def place_of(index):
+        return (index // col_count, lax.rem(index, col_count))
 
     def col_source(step):
         return lax.rem(c + col_count - step, col_count)
@@ -78,10 +85,15 @@
         loads.append(copy)
 
     barrier = pltpu.get_barrier_semaphore()
-    each(1, row_count, lambda s: pl.semaphore_signal(
-        barrier, inc=1, device_id=(row_peer(s), c), device_id_type=MESH))
-    each(1, col_count, lambda s: pl.semaphore_signal(
-        barrier, inc=1, device_id=(r, col_peer(s)), device_id_type=MESH))
+    if direct:
+        each(1, total_count, lambda s: pl.semaphore_signal(
+            barrier, inc=1, device_id=place_of(any_peer(s)), device_id_type=MESH))
+    else:
+        each(1, row_count, lambda s: pl.semaphore_signal(
+            barrier, inc=1, device_id=(row_peer(s), c), device_id_type=MESH))
+        each(1, col_count, lambda s: pl.semaphore_signal(
+            barrier, inc=1, device_id=(r, col_peer(s)), device_id_type=MESH))
+    greeted = total_count - 1 if direct else row_count + col_count - 2
 
     def remote(source, target, send, recv, device):
         return pltpu.make_async_remote_copy(
@@ -104,7 +116,7 @@
         onehot[:, pl.ds(peer * slot_count, slot_count)] = hot
     outgoing[...] = mm(onehot[...], feats[...], (0, 0)).astype(BF)
 
-    pl.semaphore_wait(barrier, row_count + col_count - 2)
+    pl.semaphore_wait(barrier, greeted)
 
     def feature_copy(step):
         return to_col(step, rows_at(outgoing, col_peer(step), slot_count),
@@ -191,8 +203,21 @@
     def share_copy(step):
         return to_row(step, rows_at(grad_out, row_peer(step), share), grad_in.at[r], send_g, recv_g)
 
-    each(1, row_count, lambda s: share_copy(s).start())
-    grad_in[r] = rows_at(grad_out, r, share)[...]
+    def spread_copy(step):
+        peer = any_peer(step)
+        return remote(rows_at(grad_out, peer, PIECE), piece_in.at[me],
+                      send_c.at[step], recv_c.at[step], place_of(peer))
+
+    def gather_copy(step):
+        own = rows_at(grads_o, me, PIECE)
+        return remote(own, own, send_z.at[step], recv_z.at[step], place_of(any_peer(step)))
+
+    if direct:
+        each(1, total_count, lambda s: spread_copy(s).start())
+        piece_in[me] = rows_at(grad_out, me, PIECE)[...]
+    else:
+        each(1, row_count, lambda s: share_copy(s).start())
+        grad_in[r] = rows_at(grad_out, r, share)[...]
     bias_row[...] = mm(jnp.ones((8, node_count), BF), pre_grads)
 
     def bias_copy(step):
@@ -223,13 +248,21 @@
         return to_col(step, rows_at(piece_out, col_peer(step) % owners, piece),
                       piece_in.at[c], send_c, recv_c)
 
-    each(1, row_count, lambda s: share_copy(s).wait_recv())
-    total = grad_in[0].astype(F32)
-    for other in range(1, row_count):
-        total = total + grad_in[other].astype(F32)
-    piece_out[...] = total.astype(BF)
-    each(1, col_count, lambda s: owning(col_peer(s), lambda: piece_copy(s).start()))
-    piece_in[c] = rows_at(piece_out, c % owners, piece)[...]
+    if direct:
+        each(1, total_count, lambda s: spread_copy(s).wait_recv())
+        whole = piece_in[0].astype(F32)
+        for other in range(1, total_count):
+            whole = whole + piece_in[other].astype(F32)
+        rows_at(grads_o, me, PIECE)[...] = whole.astype(BF)
+        each(1, total_count, lambda s: gather_copy(s).start())
+    else:
+        each(1, row_count, lambda s: share_copy(s).wait_recv())
+        total = grad_in[0].astype(F32)
+        for other in range(1, row_count):
+            total = total + grad_in[other].astype(F32)
+        piece_out[...] = total.astype(BF)
+        each(1, col_count, lambda s: owning(col_peer(s), lambda: piece_copy(s).start()))
+        piece_in[c] = rows_at(piece_out, c % owners, piece)[...]
 
     each(1, row_count, lambda s: bias_copy(s).wait_recv())
     bias_total = bias_in[0]
@@ -258,7 +291,8 @@
         final_piece(c)[...] = whole.astype(BF)
         each(1, col_count, lambda s: final_copy(s).start())
 
-    owning(c, reduce_piece)
+    if not direct:
+        owning(c, reduce_piece)
 
     each(1, col_count, lambda s: back_copy(s).wait_recv())
     base_o[...] = base + mm(onehot[...], back_in[...])
@@ -268,21 +302,27 @@
         bias_total = bias_total + bias_in2[other]
     bias_o[...] = bias_total
 
-    each(1, col_count, lambda s: owning(col_source(s), lambda: final_copy(s).wait_recv()))
-
     def share_final(step):
         own = rows_at(grads_o, r, share)
         return to_row(step, own, own, send_y, recv_y)
 
-    each(1, row_count, lambda s: share_final(s).start())
-    each(1, row_count, lambda s: share_final(s).wait_recv())
-
-    for step_copy in (degree_copy, partial_copy, panel_copy, share_copy, bias_copy, share_final):
+    if direct:
+        each(1, total_count, lambda s: gather_copy(s).wait_recv())
+        for step_copy in (spread_copy, gather_copy):
+            each(1, total_count, lambda s: step_copy(s).wait_send())
+    else:
+        each(1, col_count, lambda s: owning(col_source(s), lambda: final_copy(s).wait_recv()))
+        each(1, row_count, lambda s: share_final(s).start())
+        each(1, row_count, lambda s: share_final(s).wait_recv())
+        for step_copy in (share_copy, share_final):
+            each(1, row_count, lambda s: step_copy(s).wait_send())
+        each(1, col_count, lambda s: owning(col_peer(s), lambda: piece_copy(s).wait_send()))
+        owning(c, lambda: each(1, col_count, lambda s: final_copy(s).wait_send()))
+
+    for step_copy in (degree_copy, partial_copy, panel_copy, bias_copy):
         each(1, row_count, lambda s: step_copy(s).wait_send())
     for step_copy in (feature_copy, back_copy, bias_copy2):
         each(1, col_count, lambda s: step_copy(s).wait_send())
-    each(1, col_count, lambda s: owning(col_peer(s), lambda: piece_copy(s).wait_send()))
-    owning(c, lambda: each(1, col_count, lambda s: final_copy(s).wait_send()))
 
 
 def write_kernel(hidden_i, base_i, grads_i, bias_i, hidden, base, self_grads, neigh_grads, bias):
@@ -308,6 +348,9 @@
     grad_rows = 4 * width
     share = grad_rows // row_count
     piece = max(PIECE, share // col_count)
+    total = row_count * col_count
+    pieces = total if total * PIECE == grad_rows else col_count
+    piece_sems = pltpu.SemaphoreType.DMA((pieces,))
     bias_term = bias_term.reshape(1, hid)
     arrays = (node_feats, send_rows, send_count, block_tiles, block_values, w_self, w_neigh,
               bias_term, cotangent)
@@ -335,11 +378,11 @@
         pltpu.VMEM((received, width), BF),
         pltpu.VMEM((received, width), BF),
         pltpu.VMEM((share, half), BF),
-        pltpu.VMEM((col_count, piece, half), BF),
+        pltpu.VMEM((pieces, piece, half), BF),
         pltpu.SemaphoreType.DMA((len(arrays),)),
         col_sems, col_sems, row_sems, row_sems, row_sems, row_sems, row_sems, row_sems,
-        row_sems, row_sems, row_sems, row_sems, col_sems, col_sems, col_sems, col_sems,
-        col_sems, col_sems, col_sems, col_sems, row_sems, row_sems,
+        row_sems, row_sems, row_sems, row_sems, col_sems, col_sems, piece_sems, piece_sems,
+        col_sems, col_sems, col_sems, col_sems, row_sems, row_sems, piece_sems, piece_sems,
     ]
     results = pl.pallas_call(
         functools.partial(layer_kernel, row_count, col_count),
@@ -349,12 +392,12 @@
             jax.ShapeDtypeStruct((grad_rows, half), BF),
             jax.ShapeDtypeStruct((8, hid), F32),
         ),
-        in_specs=[pl.BlockSpec(memory_space=pl.ANY)] * len(arrays),
+        in_specs=[pl.BlockSpec(memory_space=pltpu.HBM)] * len(arrays),
         out_specs=(vmem,) * 4,
         scratch_shapes=scratch,
         compiler_params=pltpu.CompilerParams(
             collective_id=0, has_side_effects=True, vmem_limit_bytes=40 * 1024 * 1024),
-    )(*arrays)
+    )(*[pltpu.with_memory_space_constraint(a, pltpu.HBM) for a in arrays])
     hidden, input_grads, self_grads, neigh_grads, bias_grads = pl.pallas_call(
         write_kernel,
         out_shape=(
@@ -366,6 +409,7 @@
         ),
         in_specs=[vmem] * 4,
         out_specs=(vmem,) * 5,
+        compiler_params=pltpu.CompilerParams(vmem_limit_bytes=4 * 1024 * 1024),
     )(*results)
     return hidden, input_grads, self_grads, neigh_grads, bias_grads.reshape(hid)
 

time: 42.4 us -> 31.4 us (0.74)
  local copies, waits for them, and re-layouts: 8.88 us -> 0 us
  Pallas kernels: 32.4 us -> 30.6 us
    unnamed x26 -> x0, local copies, waits for them, and re-layouts: 8.88 us -> none
    pallas_call x1, Pallas kernels: 1.73 us -> 0.77 us  [shards(): pl.pallas_call(write_kernel, out_shape=(jax.ShapeDtypeStruct((nodes, hid)...]
    pallas_call x1, Pallas kernels: 30.7 us -> 29.8 us  [shards(): pl.pallas_call(functools.partial(layer_kernel, row_count, col_count), out...]
where the time goes in v2:
time: 31.4 us; the launch traced here: 31.2 us
  Pallas kernels  30.6 us (97%)
  between operations  0.64 us (2%)
    pallas_call x1, Pallas kernels, shards(): pl.pallas_call(functools.partial(layer_kernel, row_count, col_count), out...  29.8 us
    pallas_call x1, Pallas kernels, shards(): pl.pallas_call(write_kernel, out_shape=(jax.ShapeDtypeStruct((nodes, hid)...  0.77 us

profile of v2, /device:TPU:0, one launch (start us, length us, event | category | flops | bytes accessed | tf_op | source)
XLA Modules:
  0.0 31.2 jit_solution(7915193933983047715)
XLA Ops:
  0.6 29.8 %shard_map.128 = (bf16[128,256]{1,0:T(8,128)(2,1)S(1)}, f32[128,128]{1,0:T(8,128)S(1)}, bf16[512,128]{1,0:T(8,128)(2,1)S(1)}, f32[8,256]{1,0:T(8,128)S(1)}) custom-call(bf16[128,128]{1,0:T(8,128)(2,1)} %feats_h.1, s32[1,1,8,32]{3,2,1,0:T(8,128)} %rows_h.1, s32[1,1,8]{2,1,0:T(1,128)} %count_h.1, s32[1,1,4,5]{3,2,1,0:T(4,128)} %tiles_h.1, ...), custom_call_target="tpu_custom_call" | custom-call | tf_op jit(solution)/shard_map/pallas_call | solution.py:387
  30.5 0.8 %shard_map.129 = (bf16[128,256]{1,0:T(8,128)(2,1)}, f32[128,128]{1,0:T(8,128)}, f32[128,256]{1,0:T(8,128)}, f32[128,256]{1,0:T(8,128)}, f32[1,256]{1,0:T(1,128)}) custom-call(bf16[128,256]{1,0:T(8,128)(2,1)S(1)} %get-tuple-element.14.hidden_i, f32[128,128]{1,0:T(8,128)S(1)} %get-tuple-element.15.base_i, bf16[512,128]{1,0:T(8,128)(2,1)S(1)} %get-tuple-element.16.grads_i, ...), custom_call_target="tpu_custom_call" | custom-call | tf_op jit(solution)/shard_map/pallas_call | solution.py:401

commit v3 on v2

--- a/solution.py
+++ b/solution.py
@@ -20,8 +20,8 @@
 
 
 def each(first, count, body):
-    if count - first <= 32:
-        for step in range(first, count):
+    if count - first <= 8:
+        for step in sorted(range(first, count), key=lambda s: -min(s, count - s)):
             body(step)
     else:
         lax.fori_loop(first, count, lambda step, carry: (body(step), carry)[1], 0)
@@ -38,11 +38,11 @@
     feats_h, rows_h, count_h, tiles_h, values_h, w_self_h, w_neigh_h, bias_h, cot_h,
     hidden_o, base_o, grads_o, bias_o,
     feats, rows, count, tiles, values, w_self, w_neigh, bias, cot,
-    onehot, outgoing, inbox, weights, weights_t, deg_out, deg_in, part_out, part_in,
-    panel, grad_out, grad_in, bias_row, bias_in, bias_col, bias_in2, back_out, back_in,
+    feats_t, onehot, outgoing, inbox, weights, weights_t, deg_out, deg_in, part_out, part_in,
+    panel, grad_out, grad_in, back_out, back_in,
     piece_out, piece_in,
     load_sem, send_a, recv_a, send_d, recv_d, send_p, recv_p, send_m, recv_m, send_g, recv_g,
-    send_b, recv_b, send_t, recv_t, send_c, recv_c, send_h, recv_h, send_x, recv_x, send_y, recv_y, send_z, recv_z,
+    send_t, recv_t, send_c, recv_c, send_x, recv_x, send_y, recv_y, send_z, recv_z,
 ):
     node_count, in_width = feats.shape
     slot_count = rows.shape[3]
@@ -65,14 +65,25 @@
 
     me = r * col_count + c
 
-    def any_peer(step):
-        return lax.rem(me + step, total_count)
-
-    def place_of(index):
-        return (index // col_count, lax.rem(index, col_count))
-
-    def col_source(step):
-        return lax.rem(c + col_count - step, col_count)
+    others = []
+    if direct:
+        row_peers = [row_peer(step) for step in range(row_count)]
+        col_peers = [col_peer(step) for step in range(col_count)]
+        for col_step in sorted(range(col_count), key=lambda s: -min(s, col_count - s)):
+            for row_step in range(row_count):
+                if row_step or col_step:
+                    others.append((row_peers[row_step], col_peers[col_step]))
+
+    barrier = pltpu.get_barrier_semaphore()
+    if direct:
+        for place in others:
+            pl.semaphore_signal(barrier, inc=1, device_id=place, device_id_type=MESH)
+    else:
+        each(1, row_count, lambda s: pl.semaphore_signal(
+            barrier, inc=1, device_id=(row_peer(s), c), device_id_type=MESH))
+        each(1, col_count, lambda s: pl.semaphore_signal(
+            barrier, inc=1, device_id=(r, col_peer(s)), device_id_type=MESH))
+    greeted = total_count - 1 if direct else row_count + col_count - 2
 
     loads = []
     pairs = (
@@ -84,27 +95,20 @@
         copy.start()
         loads.append(copy)
 
-    barrier = pltpu.get_barrier_semaphore()
-    if direct:
-        each(1, total_count, lambda s: pl.semaphore_signal(
-            barrier, inc=1, device_id=place_of(any_peer(s)), device_id_type=MESH))
-    else:
-        each(1, row_count, lambda s: pl.semaphore_signal(
-            barrier, inc=1, device_id=(row_peer(s), c), device_id_type=MESH))
-        each(1, col_count, lambda s: pl.semaphore_signal(
-            barrier, inc=1, device_id=(r, col_peer(s)), device_id_type=MESH))
-    greeted = total_count - 1 if direct else row_count + col_count - 2
-
     def remote(source, target, send, recv, device):
         return pltpu.make_async_remote_copy(
             src_ref=source, dst_ref=target, send_sem=send, recv_sem=recv,
             device_id=device, device_id_type=MESH)
 
-    def to_row(step, source, target, send, recv):
-        return remote(source, target, send.at[step], recv.at[step], (row_peer(step), c))
-
-    def to_col(step, source, target, send, recv):
-        return remote(source, target, send.at[step], recv.at[step], (r, col_peer(step)))
+    def to_row(step, source, target, send, recv, slot=0):
+        return remote(source, target, send.at[slot], recv.at[slot], (row_peer(step), c))
+
+    def to_col(step, source, target, send, recv, slot=0):
+        return remote(source, target, send.at[slot], recv.at[slot], (r, col_peer(step)))
+
+    def take(ref, length, sem):
+        part = ref.at[pl.ds(0, length)]
+        pltpu.make_async_copy(part, part, sem.at[0]).wait()
 
     for copy in loads[:3]:
         copy.wait()
@@ -155,14 +159,15 @@
     for copy in loads[5:]:
         copy.wait()
     own_part = mm(feats[...], w_self[...]) + bias[...]
-    each(1, row_count, lambda s: degree_copy(s).wait_recv())
+    feats_t[...] = feats[...].astype(F32).T.astype(BF)
+    take(deg_in, row_count - 1, recv_d)
     degree = deg_in[0]
     for other in range(1, row_count):
         degree = degree + deg_in[other]
     inverse = 1.0 / jnp.maximum(degree[0:1, :], 1.0)
     inverse = jnp.broadcast_to(inverse, (128, 128)).T
 
-    each(1, col_count, lambda s: feature_copy(s).wait_recv())
+    take(inbox, (col_count - 1) * slot_count, recv_a)
 
     def partial_copy(step):
         return to_row(step, rows_at(part_out, row_peer(step), 128), part_in.at[r], send_p, recv_p)
@@ -176,7 +181,9 @@
     each(1, row_count, aggregate)
     agg_sum = mm(rows_at(weights, r, 128)[...], inbox[...])
     part_in[r] = jnp.zeros((128, in_width), BF)
-    each(1, row_count, lambda s: partial_copy(s).wait_recv())
+    take(inbox, (col_count - 1) * slot_count, send_a)
+    take(deg_in, row_count - 1, send_d)
+    take(part_in, row_count - 1, recv_p)
     for other in range(row_count):
         agg_sum = agg_sum + part_in[other].astype(F32)
 
@@ -186,57 +193,74 @@
     pre_grads = (
         cot[...].astype(F32) * sigmoid_pre * (1.0 + preact * (1.0 - sigmoid_pre))
     ).astype(BF)
-    rows_at(panel, r, 128)[...] = (mm(pre_grads, w_neigh[...], (1, 1)) * inverse).astype(BF)
+    tile_row = lax.broadcasted_iota(jnp.int32, (PIECE, in_width), 0)
+
+    def pack(first, second):
+        value = jnp.where(tile_row % 2 == 0, first, second)
+        high = value.astype(BF).astype(F32)
+        return jnp.where(tile_row < 2, high, value - high).astype(BF)
+
+    def unpack(packed, length):
+        total = packed[0, pl.ds(length, PIECE), :].astype(F32)
+        for other in range(1, packed.shape[0]):
+            total = total + packed[other, pl.ds(length, PIECE), :].astype(F32)
+        return total[0:1] + total[2:3], total[1:2] + total[3:4]
+
+    bias_sum = mm(jnp.ones((8, node_count), BF), pre_grads)
+    panel[r, pl.ds(128, PIECE), :] = pack(bias_sum[0:1, :in_width], bias_sum[0:1, in_width:])
+    panel[r, pl.ds(0, 128), :] = (mm(pre_grads, w_neigh[...], (1, 1)) * inverse).astype(BF)
 
     def panel_copy(step):
-        return to_row(step, rows_at(panel, r, 128), rows_at(panel, r, 128), send_m, recv_m)
+        return to_row(step, panel.at[r], panel.at[r], send_m, recv_m)
 
     each(1, row_count, lambda s: panel_copy(s).start())
 
     half = grad_out.shape[1]
-    for number, left in enumerate((feats[...], neigh_mean)):
-        product = mm(left, pre_grads, (0, 0)).astype(BF)
+    for number, (left, axis) in enumerate(((feats_t[...], 1), (neigh_mean, 0))):
+        product = mm(left, pre_grads, (axis, 0)).astype(BF)
         for side in range(2):
             grad_out[pl.ds((2 * number + side) * in_width, in_width), :] = (
                 product[:, side * half:(side + 1) * half])
 
     def share_copy(step):
-        return to_row(step, rows_at(grad_out, row_peer(step), share), grad_in.at[r], send_g, recv_g)
-
-    def spread_copy(step):
-        peer = any_peer(step)
-        return remote(rows_at(grad_out, peer, PIECE), piece_in.at[me],
-                      send_c.at[step], recv_c.at[step], place_of(peer))
-
-    def gather_copy(step):
+        return to_row(step, rows_at(grad_out, row_peer(step), share), grad_in.at[r], send_g, recv_g, step)
+
+    def spread_copy(place):
+        owner = place[0] * col_count + place[1]
+        return remote(rows_at(grad_out, owner, PIECE), piece_in.at[me],
+                      send_c.at[0], recv_c.at[0], place)
+
+    def gather_copy(place):
         own = rows_at(grads_o, me, PIECE)
-        return remote(own, own, send_z.at[step], recv_z.at[step], place_of(any_peer(step)))
+        return remote(own, own, send_z.at[0], recv_z.at[0], place)
 
     if direct:
-        each(1, total_count, lambda s: spread_copy(s).start())
+        for place in others:
+            spread_copy(place).start()
         piece_in[me] = rows_at(grad_out, me, PIECE)[...]
     else:
         each(1, row_count, lambda s: share_copy(s).start())
         grad_in[r] = rows_at(grad_out, r, share)[...]
-    bias_row[...] = mm(jnp.ones((8, node_count), BF), pre_grads)
-
-    def bias_copy(step):
-        return to_row(step, bias_row, bias_in.at[r], send_b, recv_b)
-
-    each(1, row_count, lambda s: bias_copy(s).start())
-    bias_in[r] = bias_row[...]
     hidden_o[...] = (preact * sigmoid_pre).astype(BF)
     base = mm(pre_grads, w_self[...], (1, 1))
 
-    each(1, row_count, lambda s: panel_copy(s).wait_recv())
-    back_out[...] = mm(weights_t[...], panel[...]).astype(BF)
+    take(part_in, row_count - 1, send_p)
+    take(panel, row_count - 1, recv_m)
+    returned = mm(weights_t[:, pl.ds(0, 128)], panel[0, pl.ds(0, 128), :])
+    for other in range(1, row_count):
+        returned = returned + mm(
+            weights_t[:, pl.ds(other * 128, 128)], panel[other, pl.ds(0, 128), :])
+    returned = returned.astype(BF)
+    bias_tile = pack(*unpack(panel, 128))
+    for peer in range(col_count):
+        back_out[peer, pl.ds(0, slot_count), :] = returned[peer * slot_count:(peer + 1) * slot_count]
+        back_out[peer, pl.ds(slot_count, PIECE), :] = bias_tile
 
     def back_copy(step):
-        return to_col(step, rows_at(back_out, col_peer(step), slot_count),
-                      rows_at(back_in, c, slot_count), send_t, recv_t)
+        return to_col(step, back_out.at[col_peer(step)], back_in.at[c], send_t, recv_t)
 
     each(1, col_count, lambda s: back_copy(s).start())
-    rows_at(back_in, c, slot_count)[...] = rows_at(back_out, c, slot_count)[...]
+    back_in[c] = back_out[c]
 
     def owning(holder, body):
         if owners == col_count:
@@ -246,15 +270,16 @@
 
     def piece_copy(step):
         return to_col(step, rows_at(piece_out, col_peer(step) % owners, piece),
-                      piece_in.at[c], send_c, recv_c)
+                      piece_in.at[c], send_c, recv_c, step)
 
     if direct:
-        each(1, total_count, lambda s: spread_copy(s).wait_recv())
+        take(piece_in, total_count - 1, recv_c)
         whole = piece_in[0].astype(F32)
         for other in range(1, total_count):
             whole = whole + piece_in[other].astype(F32)
         rows_at(grads_o, me, PIECE)[...] = whole.astype(BF)
-        each(1, total_count, lambda s: gather_copy(s).start())
+        for place in others:
+            gather_copy(place).start()
     else:
         each(1, row_count, lambda s: share_copy(s).wait_recv())
         total = grad_in[0].astype(F32)
@@ -264,24 +289,12 @@
         each(1, col_count, lambda s: owning(col_peer(s), lambda: piece_copy(s).start()))
         piece_in[c] = rows_at(piece_out, c % owners, piece)[...]
 
-    each(1, row_count, lambda s: bias_copy(s).wait_recv())
-    bias_total = bias_in[0]
-    for other in range(1, row_count):
-        bias_total = bias_total + bias_in[other]
-    bias_col[...] = bias_total
-
-    def bias_copy2(step):
-        return to_col(step, bias_col, bias_in2.at[c], send_h, recv_h)
-
-    each(1, col_count, lambda s: bias_copy2(s).start())
-    bias_in2[c] = bias_col[...]
-
     def final_piece(holder):
         start = r * share + holder * piece
         return grads_o.at[pl.ds(pl.multiple_of(start, piece), piece)]
 
     def final_copy(step):
-        return to_col(step, final_piece(c), final_piece(c), send_x, recv_x)
+        return to_col(step, final_piece(c), final_piece(c), send_x, recv_x, step)
 
     def reduce_piece():
         each(1, col_count, lambda s: piece_copy(s).wait_recv())
@@ -294,35 +307,31 @@
     if not direct:
         owning(c, reduce_piece)
 
-    each(1, col_count, lambda s: back_copy(s).wait_recv())
-    base_o[...] = base + mm(onehot[...], back_in[...])
-    each(1, col_count, lambda s: bias_copy2(s).wait_recv())
-    bias_total = bias_in2[0]
-    for other in range(1, col_count):
-        bias_total = bias_total + bias_in2[other]
-    bias_o[...] = bias_total
+    take(back_in, col_count - 1, recv_t)
+    arrived = jnp.concatenate(
+        [back_in[peer, pl.ds(0, slot_count), :] for peer in range(col_count)], axis=0)
+    base_o[...] = base + mm(onehot[...], arrived)
+    bias_o[...] = jnp.broadcast_to(
+        jnp.concatenate(unpack(back_in, slot_count), axis=1), bias_o.shape)
+    take(panel, row_count - 1, send_m)
+    take(back_in, col_count - 1, send_t)
 
     def share_final(step):
         own = rows_at(grads_o, r, share)
-        return to_row(step, own, own, send_y, recv_y)
+        return to_row(step, own, own, send_y, recv_y, step)
 
     if direct:
-        each(1, total_count, lambda s: gather_copy(s).wait_recv())
-        for step_copy in (spread_copy, gather_copy):
-            each(1, total_count, lambda s: step_copy(s).wait_send())
+        take(piece_in, total_count - 1, send_c)
+        take(grads_o, (total_count - 1) * PIECE, send_z)
+        take(grads_o, (total_count - 1) * PIECE, recv_z)
     else:
-        each(1, col_count, lambda s: owning(col_source(s), lambda: final_copy(s).wait_recv()))
+        each(1, col_count, lambda s: owning(lax.rem(c + col_count - s, col_count), lambda: final_copy(s).wait_recv()))
         each(1, row_count, lambda s: share_final(s).start())
         each(1, row_count, lambda s: share_final(s).wait_recv())
         for step_copy in (share_copy, share_final):
             each(1, row_count, lambda s: step_copy(s).wait_send())
         each(1, col_count, lambda s: owning(col_peer(s), lambda: piece_copy(s).wait_send()))
         owning(c, lambda: each(1, col_count, lambda s: final_copy(s).wait_send()))
-
-    for step_copy in (degree_copy, partial_copy, panel_copy, bias_copy):
-        each(1, row_count, lambda s: step_copy(s).wait_send())
-    for step_copy in (feature_copy, back_copy, bias_copy2):
-        each(1, col_count, lambda s: step_copy(s).wait_send())
 
 
 def write_kernel(hidden_i, base_i, grads_i, bias_i, hidden, base, self_grads, neigh_grads, bias):
@@ -359,6 +368,7 @@
     col_sems = pltpu.SemaphoreType.DMA((col_count,))
     vmem = pl.BlockSpec(memory_space=pltpu.VMEM)
     scratch = [space(array.shape, array.dtype) for space, array in zip(spaces, arrays)] + [
+        pltpu.VMEM((width, nodes), BF),
         pltpu.VMEM((nodes, received), BF),
         pltpu.VMEM((received, width), BF),
         pltpu.VMEM((received, width), BF),
@@ -368,21 +378,17 @@
         pltpu.VMEM((row_count, 8, nodes), F32),
         pltpu.VMEM((panel, width), BF),
         pltpu.VMEM((row_count, nodes, width), BF),
-        pltpu.VMEM((panel, width), BF),
+        pltpu.VMEM((row_count, nodes + PIECE, width), BF),
         pltpu.VMEM((grad_rows, half), BF),
         pltpu.VMEM((row_count, share, half), BF),
-        pltpu.VMEM((8, hid), F32),
-        pltpu.VMEM((row_count, 8, hid), F32),
-        pltpu.VMEM((8, hid), F32),
-        pltpu.VMEM((col_count, 8, hid), F32),
-        pltpu.VMEM((received, width), BF),
-        pltpu.VMEM((received, width), BF),
+        pltpu.VMEM((col_count, slots + PIECE, width), BF),
+        pltpu.VMEM((col_count, slots + PIECE, width), BF),
         pltpu.VMEM((share, half), BF),
         pltpu.VMEM((pieces, piece, half), BF),
         pltpu.SemaphoreType.DMA((len(arrays),)),
         col_sems, col_sems, row_sems, row_sems, row_sems, row_sems, row_sems, row_sems,
-        row_sems, row_sems, row_sems, row_sems, col_sems, col_sems, piece_sems, piece_sems,
-        col_sems, col_sems, col_sems, col_sems, row_sems, row_sems, piece_sems, piece_sems,
+        row_sems, row_sems, col_sems, col_sems, piece_sems, piece_sems,
+        col_sems, col_sems, row_sems, row_sems, piece_sems, piece_sems,
     ]
     results = pl.pallas_call(
         functools.partial(layer_kernel, row_count, col_count),

time: 31.4 us -> 30.7 us (0.978)
  Pallas kernels: 30.6 us -> 29.8 us
    pallas_call x1, Pallas kernels: 29.8 us -> 29.1 us  [shards(): pl.pallas_call(functools.partial(layer_kernel, row_count, col_count), out...]
where the time goes in v3:
time: 30.7 us; the launch traced here: 30.5 us
  Pallas kernels  29.8 us (97%)
  between operations  0.64 us (2%)
    pallas_call x1, Pallas kernels, shards(): pl.pallas_call(functools.partial(layer_kernel, row_count, col_count), out...  29.1 us
    pallas_call x1, Pallas kernels, shards(): pl.pallas_call(write_kernel, out_shape=(jax.ShapeDtypeStruct((nodes, hid)...  0.77 us

profile of v3, /device:TPU:0, one launch (start us, length us, event | category | flops | bytes accessed | tf_op | source)
XLA Modules:
  0.0 30.5 jit_solution(11386913189545041268)
XLA Ops:
  0.6 29.1 %shard_map.128 = (bf16[128,256]{1,0:T(8,128)(2,1)S(1)}, f32[128,128]{1,0:T(8,128)S(1)}, bf16[512,128]{1,0:T(8,128)(2,1)S(1)}, f32[8,256]{1,0:T(8,128)S(1)}) custom-call(bf16[128,128]{1,0:T(8,128)(2,1)} %feats_h.1, s32[1,1,8,32]{3,2,1,0:T(8,128)} %rows_h.1, s32[1,1,8]{2,1,0:T(1,128)} %count_h.1, s32[1,1,4,5]{3,2,1,0:T(4,128)} %tiles_h.1, ...), custom_call_target="tpu_custom_call" | custom-call | tf_op jit(solution)/shard_map/pallas_call | solution.py:393
  29.7 0.8 %shard_map.129 = (bf16[128,256]{1,0:T(8,128)(2,1)}, f32[128,128]{1,0:T(8,128)}, f32[128,256]{1,0:T(8,128)}, f32[128,256]{1,0:T(8,128)}, f32[1,256]{1,0:T(1,128)}) custom-call(bf16[128,256]{1,0:T(8,128)(2,1)S(1)} %get-tuple-element.14.hidden_i, f32[128,128]{1,0:T(8,128)S(1)} %get-tuple-element.15.base_i, bf16[512,128]{1,0:T(8,128)(2,1)S(1)} %get-tuple-element.16.grads_i, ...), custom_call_target="tpu_custom_call" | custom-call | tf_op jit(solution)/shard_map/pallas_call | solution.py:407

commit v4 on v3

--- a/solution.py
+++ b/solution.py
@@ -69,7 +69,7 @@
     if direct:
         row_peers = [row_peer(step) for step in range(row_count)]
         col_peers = [col_peer(step) for step in range(col_count)]
-        for col_step in sorted(range(col_count), key=lambda s: -min(s, col_count - s)):
+        for col_step in range(col_count):
             for row_step in range(row_count):
                 if row_step or col_step:
                     others.append((row_peers[row_step], col_peers[col_step]))
@@ -241,7 +241,6 @@
     else:
         each(1, row_count, lambda s: share_copy(s).start())
         grad_in[r] = rows_at(grad_out, r, share)[...]
-    hidden_o[...] = (preact * sigmoid_pre).astype(BF)
     base = mm(pre_grads, w_self[...], (1, 1))
 
     take(part_in, row_count - 1, send_p)
@@ -313,6 +312,7 @@
     base_o[...] = base + mm(onehot[...], arrived)
     bias_o[...] = jnp.broadcast_to(
         jnp.concatenate(unpack(back_in, slot_count), axis=1), bias_o.shape)
+    hidden_o[...] = (preact * sigmoid_pre).astype(BF)
     take(panel, row_count - 1, send_m)
     take(back_in, col_count - 1, send_t)
 

time: 30.7 us -> 29 us (0.945)
  Pallas kernels: 29.8 us -> 28.1 us
    pallas_call x1, Pallas kernels: 29.1 us -> 27.4 us  [shards(): pl.pallas_call(functools.partial(layer_kernel, row_count, col_count), out...]
where the time goes in v4:
time: 29 us; the launch traced here: 28.8 us
  Pallas kernels  28.1 us (97%)
  between operations  0.64 us (2%)
    pallas_call x1, Pallas kernels, shards(): pl.pallas_call(functools.partial(layer_kernel, row_count, col_count), out...  27.4 us
    pallas_call x1, Pallas kernels, shards(): pl.pallas_call(write_kernel, out_shape=(jax.ShapeDtypeStruct((nodes, hid)...  0.77 us

profile of v4, /device:TPU:0, one launch (start us, length us, event | category | flops | bytes accessed | tf_op | source)
XLA Modules:
  0.0 28.8 jit_solution(9582505290592044200)
XLA Ops:
  0.6 27.4 %shard_map.128 = (bf16[128,256]{1,0:T(8,128)(2,1)S(1)}, f32[128,128]{1,0:T(8,128)S(1)}, bf16[512,128]{1,0:T(8,128)(2,1)S(1)}, f32[8,256]{1,0:T(8,128)S(1)}) custom-call(bf16[128,128]{1,0:T(8,128)(2,1)} %feats_h.1, s32[1,1,8,32]{3,2,1,0:T(8,128)} %rows_h.1, s32[1,1,8]{2,1,0:T(1,128)} %count_h.1, s32[1,1,4,5]{3,2,1,0:T(4,128)} %tiles_h.1, ...), custom_call_target="tpu_custom_call" | custom-call | tf_op jit(solution)/shard_map/pallas_call | solution.py:393
  28.0 0.8 %shard_map.129 = (bf16[128,256]{1,0:T(8,128)(2,1)}, f32[128,128]{1,0:T(8,128)}, f32[128,256]{1,0:T(8,128)}, f32[128,256]{1,0:T(8,128)}, f32[1,256]{1,0:T(1,128)}) custom-call(bf16[128,256]{1,0:T(8,128)(2,1)S(1)} %get-tuple-element.14.hidden_i, f32[128,128]{1,0:T(8,128)S(1)} %get-tuple-element.15.base_i, bf16[512,128]{1,0:T(8,128)(2,1)S(1)} %get-tuple-element.16.grads_i, ...), custom_call_target="tpu_custom_call" | custom-call | tf_op jit(solution)/shard_map/pallas_call | solution.py:407
